TPU v7x, 128 devices: a whole 4x4x4 slice. The times are simulated.
128 devices in a mesh: dp: 8 (over x, z_hi), vocab: 16 (over z_lo, y, core).
Axes of the slice: x: 4, y: 4, z: 4 (z_hi: 2, z_lo: 2; z = z_hi * 2 + z_lo), core: 2. Of those that a mesh axis runs over, the one named last changes fastest.
Arguments:
- query_hidden: bfloat16 [16, 128, 4096], P('dp', None, 'vocab'), may hold values from -144 to 144
- passage_hidden: bfloat16 [16, 256, 4096], P('dp', None, 'vocab'), may hold values from -144 to 144
- head_weight: bfloat16 [4096, 32768], P(None, 'vocab'), may hold values from -6 to 6
- query_mask: int32 [16, 128], P('dp'), may hold values from 0 to 1, as said below
- passage_mask: int32 [16, 256], P('dp'), may hold values from 0 to 1, as said below
- positive: int32 [16], replicated, may hold values from 0 to 15
Outputs:
- grad_query_hidden: bfloat16 [16, 128, 4096], P('dp', None, 'vocab')
- grad_passage_hidden: bfloat16 [16, 256, 4096], P('dp', None, 'vocab')
- query_loss: float32 [16], P('dp')
Inputs may be any that keep to these rules, and one draw needn't show every extreme that they name: `query_mask`: the live tokens of each query are a prefix of 32 to 128 positions. `passage_mask`: the live tokens of each passage are a prefix of 64 to 256 positions.
All inputs are finite; a program needn't handle non-finite values.
Results may differ from a plain program's by a relative error of at most 0.0095.
Values may be sent and summed in bfloat16 or wider, within the bound.
No kernel may reach another device: no remote copies, remote signals or barrier semaphores. Data moves between devices by JAX's collectives and lax.ppermute only.
A program may use at most 128 MiB of HBM per device.

v0:
```python
import jax
import jax.numpy as jnp
from jax import lax
from jax.sharding import PartitionSpec as P

normalizer_sharpness = 0.2
score_div = 16.0
loss_scale = 65536.0


def pooling_row_block(lexicon_projection_lines, live):
    divided_similarity_matrix = lexicon_projection_lines / normalizer_sharpness
    live_rows = live[:, :, None] > 0
    largest_element = jnp.max(jnp.where(live_rows, divided_similarity_matrix, -1e30), axis=1)
    expo = jnp.where(
        live_rows, jnp.exp(divided_similarity_matrix - largest_element[:, None, :]), 0.0
    )
    cumulative_accumulator = jnp.sum(expo, axis=1)
    softened_rectifier_output = normalizer_sharpness * (
        largest_element + jnp.log(cumulative_accumulator)
    )
    return (softened_rectifier_output, expo / cumulative_accumulator[:, None, :])


def exact_dot(left, right):
    return jnp.dot(left, right, precision=lax.Precision.HIGHEST, preferred_element_type=jnp.float32)


def loss_and_grad(scores, targets, total_queries):
    largest_element = jnp.max(scores, axis=1)
    lse = largest_element + jnp.log(jnp.sum(jnp.exp(scores - largest_element[:, None]), axis=1))
    picked = (targets[:, None] == jnp.arange(scores.shape[1], dtype=jnp.int32)[None, :]).astype(
        jnp.float32
    )
    losses = lse - jnp.sum(scores * picked, axis=1)
    probs = jnp.exp(scores - lse[:, None])
    return (losses, (probs - picked) * (loss_scale / total_queries))


def token_grads(dpooled, softened_rectifier_output, share):
    dsmooth = dpooled * jnp.where(
        softened_rectifier_output > 0,
        1.0 / (1.0 + jnp.maximum(softened_rectifier_output, 0.0)),
        0.0,
    )
    dlogits = (share * dsmooth[:, None, :]).astype(jnp.bfloat16)
    return dlogits.reshape(dlogits.shape[0] * dlogits.shape[1], dlogits.shape[2])


def on_device(query_hidden, passage_hidden, head_weight, query_mask, passage_mask, positive):
    q_count, q_len, width_part = query_hidden.shape
    p_count, p_len, _ = passage_hidden.shape
    columns = head_weight.shape[1]
    split = q_count * q_len
    tokens = jnp.concatenate(
        [
            query_hidden.reshape(split, width_part),
            passage_hidden.reshape(p_count * p_len, width_part),
        ],
        axis=0,
    )
    w_rows = head_weight
    lexicon_projection_lines = jnp.dot(
        lax.all_gather(tokens, "vocab", axis=1, tiled=True),
        w_rows,
        preferred_element_type=jnp.float32,
    )
    q_smooth, q_share = pooling_row_block(
        lexicon_projection_lines[:split].reshape(q_count, q_len, columns), query_mask
    )
    p_smooth, p_share = pooling_row_block(
        lexicon_projection_lines[split:].reshape(p_count, p_len, columns), passage_mask
    )
    q_pooled = jnp.log1p(jnp.maximum(q_smooth, 0.0))
    p_pooled = jnp.log1p(jnp.maximum(p_smooth, 0.0))
    group = lax.axis_index("dp")
    total_queries = positive.shape[0]
    p_every = lax.all_gather(p_pooled, "dp", axis=0, tiled=True)
    scores = lax.psum(exact_dot(q_pooled, p_every.T), "vocab") / score_div
    targets = lax.dynamic_slice_in_dim(positive, group * q_count, q_count, 0)
    query_loss, dscores = loss_and_grad(scores, targets, total_queries)
    dq_pooled = exact_dot(dscores, p_every) / score_div
    grad_passage_summary = lax.psum_scatter(
        exact_dot(dscores.T, q_pooled) / score_div, "dp", scatter_dimension=0, tiled=True
    )
    dlogits = jnp.concatenate(
        [
            token_grads(dq_pooled, q_smooth, q_share),
            token_grads(grad_passage_summary, p_smooth, p_share),
        ],
        axis=0,
    )
    w_rows = head_weight
    own_grad = lax.psum_scatter(
        lax.dot_general(
            w_rows, dlogits, (((1,), (1,)), ((), ())), preferred_element_type=jnp.float32
        ),
        "vocab",
        scatter_dimension=0,
        tiled=True,
    ).T
    own_grad = own_grad.astype(jnp.bfloat16)
    grad_query_hidden = own_grad[:split].reshape(q_count, q_len, width_part)
    grad_passage_hidden = own_grad[split:].reshape(p_count, p_len, width_part)
    return (grad_query_hidden, grad_passage_hidden, query_loss)


def solution(mesh):
    return jax.shard_map(
        on_device,
        mesh=mesh,
        in_specs=(
            P("dp", None, "vocab"),
            P("dp", None, "vocab"),
            P(None, "vocab"),
            P("dp", None),
            P("dp", None),
            P(),
        ),
        out_specs=(P("dp", None, "vocab"), P("dp", None, "vocab"), P("dp")),
        check_vma=False,
    )
```

profile of v0, /device:TPU:0, one launch (start us, length us, event | category | flops | bytes accessed | tf_op | source)
XLA Modules:
  0.0 344.2 jit_solution(16631525663870407592)
XLA Ops:
  7.2 0.0 all-gather.3.cloned.1.call-start
  7.2 1.8 pad_maximum_fusion
  9.0 0.0 all-gather.3.cloned.1.call-update
  9.0 0.0 all-reduce.3.cloned.1.call-start
  9.1 0.7 broadcast_compare_fusion
  9.8 1.2 dynamic-slice
  11.7 0.7 dynamic_slice.3
  12.4 0.7 broadcast_compare_fusion.1
  13.1 0.7 fusion.29
  13.8 50.4 %all-gather.3.cloned.1.call-done = bf16[768,4096]{1,0:T(8,128)(2,1)} async-done(((bf16[768,256]{1,0:T(8,128)(2,1)}), bf16[768,4096]{1,0:T(8,128)(2,1)}) %all-gather.3.cloned.1.call-update) | async-done | bytes 6291472 | tf_op jit(solution)/shard_map/all_gather | solution.py:64
  64.2 17.7 %fusion.23 = f32[768,2048]{1,0:T(8,128)S(1)} fusion(bf16[768,4096]{1,0:T(8,128)(2,1)} %all-gather.3.cloned.1.call-done, bf16[4096,2048]{1,0:T(8,128)(2,1)} %param.8), kind=kOutput, calls=%fused_computation.53 | convolution fusion | flops 12884901888 | bytes 29360128 | tf_op jit(solution)/shard_map/dot_general | solution.py:63
  81.9 0.0 copy-start
  81.9 0.6 select_reduce_fusion.1
  82.5 0.3 select_reduce_fusion.3
  82.9 0.5 select_reduce_fusion.2
  83.3 1.2 copy-done
  84.6 0.9 select_reduce_fusion
  85.6 34.2 %all-gather = f32[8,2,2048]{2,1,0:T(2,128)S(1)} all-gather(f32[1,2,2048]{2,1,0:T(2,128)S(1)} %log-plus-one_bitcast_fusion), channel_id=1, replica_groups=mesh['dp'=8,'vocab'=16] {'dp'}, dimensions={0}, use_global_device_ids=true | all-gather | bytes 147456 | tf_op jit(solution)/shard_map/all_gather | solution.py:78
  119.8 0.1 reshape.58
  119.9 0.2 fusion.12
  120.1 27.2 %psum.7 = f32[2,16]{1,0:T(2,128)S(1)} all-reduce(f32[2,16]{1,0:T(2,128)S(1)} %fusion.12), channel_id=1, replica_groups=mesh['dp'=8,'vocab'=16] {'vocab'}, use_global_device_ids=true, to_apply=%region_4.5 | all-reduce | flops 32 | bytes 256 | tf_op jit(solution)/shard_map/psum | solution.py:79
  147.3 0.1 fusion.18
  147.4 0.2 select_reduce_fusion.4
  147.7 0.5 fusion.22
  148.2 1.1 convolution_multiply_fusion
  149.3 0.0 all-reduce.3.cloned.1.call-update
  149.3 0.2 reduce-scatter.2.cloned.1.call-start
  149.5 0.3 fusion.6
  149.8 2.2 fusion.7
  152.0 79.7 %all-reduce.3.cloned.1.call-done = f32[16,2048]{1,0:T(8,128)} async-done(((f32[16,2048]{1,0:T(8,128)}), f32[16,2048]{1,0:T(8,128)}) %all-reduce.3.cloned.1.call-update) | async-done | bytes 131088
  231.6 0.9 fusion.10
  232.5 3.0 fusion
  235.5 19.4 %convolution_bitcast_fusion = f32[4096,768]{0,1:T(8,128)} fusion(bf16[4096,2048]{1,0:T(8,128)(2,1)} %param.8, bf16[512,2048]{1,0:T(8,128)(2,1)S(1)} %fusion, bf16[256,2048]{1,0:T(8,128)(2,1)S(1)} %fusion.7), kind=kOutput, calls=%fused_computation | convolution fusion | flops 12891193344 | bytes 32505856 | tf_op jit(solution)/shard_map/dot_general | solution.py:95
  254.9 0.0 reduce-scatter.2.cloned.1.call-update
  254.9 80.2 %reduce-scatter.2.cloned.1.call-done = f32[256,768]{0,1:T(8,128)} async-done(((f32[4096,768]{0,1:T(8,128)}), f32[256,768]{0,1:T(8,128)}) %reduce-scatter.2.cloned.1.call-update) | async-done | bytes 786448 | tf_op jit(solution)/shard_map/reduce_scatter | solution.py:94
  335.1 1.2 convert_bitcast_fusion
  336.3 0.7 slice.18
  337.0 0.7 slice.19
  (2 shorter events, 0.1 us)
Async XLA Ops:
  7.2 57.0 %all-gather.3.cloned.1.call-start = ((), (), s32[]{:S(2)}) async-start(), calls=%async_computation.1 | async-start | bytes 6684672 | tf_op jit(solution)/shard_map/all_gather | solution.py:64
  9.0 222.6 %all-reduce.3.cloned.1.call-start = ((), (), s32[]{:S(2)}) async-start(), calls=%async_computation.3 | async-start | bytes 262144
  81.9 2.7 copy-start
  149.3 185.8 %reduce-scatter.2.cloned.1.call-start = ((), (), s32[]{:S(2)}) async-start(), calls=%async_computation.2 | async-start | bytes 13369344 | tf_op jit(solution)/shard_map/reduce_scatter | solution.py:94
Sparse Core Ops, SparseCore 0:
  9.6 54.5 all-gather.2
  149.4 82.1 all-reduce.2
  255.0 80.0 reduce-scatter.1
where the time goes:
time: 345 us; the launch traced here: 344 us
  waiting for transfers between devices  210 us (61%)
  blocking collectives  61.4 us (18%)
  matrix products  38.7 us (11%)
  between operations  14.5 us (4%)
  other arithmetic  14.3 us (4%)
  local copies, waits for them, and re-layouts  4.7 us (1%)
    reduce_scatter x1, waiting for transfers between devices, on_device(): lax.psum_scatter(lax.dot_general(w_rows, dlogits, (((1,), (1,)), ((), ())...  80.2 us
    unnamed x4, waiting for transfers between devices  79.7 us
    all_gather x1, waiting for transfers between devices, on_device(): lax.all_gather(tokens, 'vocab', axis=1, tiled=True)  50.4 us
    all_gather x1, blocking collectives, on_device(): p_every = lax.all_gather(p_pooled, 'dp', axis=0, tiled=True)  34.2 us
    psum x1, blocking collectives, on_device(): scores = lax.psum(exact_dot(q_pooled, p_every.T), 'vocab') / score_div  27.2 us
    dot_general x1, matrix products, on_device(): lax.dot_general(w_rows, dlogits, (((1,), (1,)), ((), ())), preferred_elem...  19.4 us
    dot_general x1, matrix products, on_device(): jnp.dot(lax.all_gather(tokens, 'vocab', axis=1, tiled=True), w_rows, pref...  17.7 us
  transfers between devices with their start and end apart: 3, of which 3 were waited for; matrix products, arithmetic and copies ran while one was open for 2% of the time, Pallas kernels for 0%

commit v1 on v0

--- a/solution.py
+++ b/solution.py
@@ -75,7 +75,11 @@
     p_pooled = jnp.log1p(jnp.maximum(p_smooth, 0.0))
     group = lax.axis_index("dp")
     total_queries = positive.shape[0]
-    p_every = lax.all_gather(p_pooled, "dp", axis=0, tiled=True)
+    queue = []
+    for _ in range(jax.lax.axis_size("dp")):
+        queue.append(p_pooled)
+    before = jax.lax.all_to_all(jnp.stack(queue), axis_name="dp", split_axis=0, concat_axis=0)
+    p_every = jnp.concatenate(before, axis=0)
     scores = lax.psum(exact_dot(q_pooled, p_every.T), "vocab") / score_div
     targets = lax.dynamic_slice_in_dim(positive, group * q_count, q_count, 0)
     query_loss, dscores = loss_and_grad(scores, targets, total_queries)

time: 345 us -> 323 us (0.936)
  blocking collectives: 61.4 us -> 27.2 us
  starting transfers between devices: 0.3 us -> 7.18 us
  waiting for transfers between devices: 210 us -> 214 us
    all_gather x1 -> x0, blocking collectives: 34.2 us -> none  [on_device(): p_every = lax.all_gather(p_pooled, 'dp', axis=0, tiled=True)]
    all_to_all x0 -> x1, starting transfers between devices: none -> 6.88 us  [on_device(): jax.lax.all_to_all(jnp.stack(queue), axis_name='dp', split_axis=0, concat...]
    all_to_all x0 -> x1, waiting for transfers between devices: none -> 5.79 us  [on_device(): jax.lax.all_to_all(jnp.stack(queue), axis_name='dp', split_axis=0, concat...]
  transfers between devices with their start and end apart: 3 -> 4, of which waited for: 3 -> 4; matrix products, arithmetic and copies ran while one was open for 2% -> 3% of each run, Pallas kernels for 0% -> 0%
where the time goes in v1:
time: 323 us; the launch traced here: 322 us
  waiting for transfers between devices  214 us (66%)
  matrix products  38.7 us (12%)
  blocking collectives  27.2 us (8%)
  other arithmetic  15.9 us (5%)
  between operations  14.5 us (4%)
  starting transfers between devices  7.18 us (2%)
  local copies, waits for them, and re-layouts  4.93 us (2%)
    reduce_scatter x1, waiting for transfers between devices, on_device(): lax.psum_scatter(lax.dot_general(w_rows, dlogits, (((1,), (1,)), ((), ())...  80.2 us
    unnamed x4, waiting for transfers between devices  77.5 us
    all_gather x1, waiting for transfers between devices, on_device(): lax.all_gather(tokens, 'vocab', axis=1, tiled=True)  50.4 us
    psum x1, blocking collectives, on_device(): scores = lax.psum(exact_dot(q_pooled, p_every.T), 'vocab') / score_div  27.2 us
    dot_general x1, matrix products, on_device(): lax.dot_general(w_rows, dlogits, (((1,), (1,)), ((), ())), preferred_elem...  19.4 us
    dot_general x1, matrix products, on_device(): jnp.dot(lax.all_gather(tokens, 'vocab', axis=1, tiled=True), w_rows, pref...  17.7 us
    all_to_all x1, starting transfers between devices, on_device(): jax.lax.all_to_all(jnp.stack(queue), axis_name='dp', split_axis=0, concat...  6.88 us
  transfers between devices with their start and end apart: 4, of which 4 were waited for; matrix products, arithmetic and copies ran while one was open for 3% of the time, Pallas kernels for 0%

profile of v1, /device:TPU:0, one launch (start us, length us, event | category | flops | bytes accessed | tf_op | source)
XLA Modules:
  0.0 322.4 jit_solution(14731936501507302420)
XLA Ops:
  7.2 0.0 all-gather.2.cloned.1.call-start
  7.2 1.8 pad_maximum_fusion
  9.0 0.0 all-gather.2.cloned.1.call-update
  9.0 0.7 broadcast_compare_fusion
  9.7 1.2 dynamic-slice
  11.6 0.7 dynamic_slice.3
  12.4 0.7 broadcast_compare_fusion.1
  13.0 0.7 fusion.29
  13.7 50.4 %all-gather.2.cloned.1.call-done = bf16[768,4096]{1,0:T(8,128)(2,1)} async-done(((bf16[768,256]{1,0:T(8,128)(2,1)}), bf16[768,4096]{1,0:T(8,128)(2,1)}) %all-gather.2.cloned.1.call-update) | async-done | bytes 6291472 | tf_op jit(solution)/shard_map/all_gather | solution.py:64
  64.2 17.7 %fusion.23 = f32[768,2048]{1,0:T(8,128)S(1)} fusion(bf16[768,4096]{1,0:T(8,128)(2,1)} %all-gather.2.cloned.1.call-done, bf16[4096,2048]{1,0:T(8,128)(2,1)} %param.8), kind=kOutput, calls=%fused_computation.53 | convolution fusion | flops 12884901888 | bytes 29360128 | tf_op jit(solution)/shard_map/dot_general | solution.py:63
  81.9 0.0 copy-start
  81.9 0.6 select_reduce_fusion.1
  82.5 0.3 select_reduce_fusion.3
  82.9 0.9 select_reduce_fusion
  83.8 0.8 copy-done
  84.6 0.7 stack.2
  85.3 6.9 %all-to-all-start = ((f32[8,2,2048]{2,1,0:T(2,128)}), f32[8,2,2048]{2,1,0:T(2,128)S(1)}, u32[]{:S(2)}, u32[]{:S(2)}) async-start(f32[8,2,2048]{2,1,0:T(2,128)} %stack.2), calls=%async_computation | async-start | bytes 262144 | tf_op jit(solution)/shard_map/all_to_all | solution.py:81
  92.2 0.0 all-reduce.3.cloned.1.call-start
  92.2 2.1 select_reduce_fusion.2
  94.3 5.8 %all-to-all-done = f32[8,2,2048]{2,1,0:T(2,128)S(1)} async-done(((f32[8,2,2048]{2,1,0:T(2,128)}), f32[8,2,2048]{2,1,0:T(2,128)S(1)}, u32[]{:S(2)}, u32[]{:S(2)}) %all-to-all-start) | async-done | bytes 131104 | tf_op jit(solution)/shard_map/all_to_all | solution.py:81
  100.1 0.1 reshape.61
  100.2 0.2 fusion.12
  100.4 27.2 %psum.7 = f32[2,16]{1,0:T(2,128)S(1)} all-reduce(f32[2,16]{1,0:T(2,128)S(1)} %fusion.12), channel_id=1, replica_groups=mesh['dp'=8,'vocab'=16] {'vocab'}, use_global_device_ids=true, to_apply=%region_4.5 | all-reduce | flops 32 | bytes 256 | tf_op jit(solution)/shard_map/psum | solution.py:83
  127.6 0.1 fusion.18
  127.7 0.2 select_reduce_fusion.4
  127.9 0.5 fusion.22
  128.5 1.1 convolution_multiply_fusion
  129.6 0.0 all-reduce.3.cloned.1.call-update
  129.6 0.2 reduce-scatter.2.cloned.1.call-start
  129.8 0.3 fusion.6
  130.1 2.2 fusion.7
  132.3 77.5 %all-reduce.3.cloned.1.call-done = f32[16,2048]{1,0:T(8,128)} async-done(((f32[16,2048]{1,0:T(8,128)}), f32[16,2048]{1,0:T(8,128)}) %all-reduce.3.cloned.1.call-update) | async-done | bytes 131088
  209.7 0.9 fusion.10
  210.6 3.0 fusion
  213.6 19.4 %convolution_bitcast_fusion = f32[4096,768]{0,1:T(8,128)} fusion(bf16[4096,2048]{1,0:T(8,128)(2,1)} %param.8, bf16[512,2048]{1,0:T(8,128)(2,1)S(1)} %fusion, bf16[256,2048]{1,0:T(8,128)(2,1)S(1)} %fusion.7), kind=kOutput, calls=%fused_computation | convolution fusion | flops 12891193344 | bytes 32505856 | tf_op jit(solution)/shard_map/dot_general | solution.py:99
  233.0 0.0 reduce-scatter.2.cloned.1.call-update
  233.0 80.2 %reduce-scatter.2.cloned.1.call-done = f32[256,768]{0,1:T(8,128)} async-done(((f32[4096,768]{0,1:T(8,128)}), f32[256,768]{0,1:T(8,128)}) %reduce-scatter.2.cloned.1.call-update) | async-done | bytes 786448 | tf_op jit(solution)/shard_map/reduce_scatter | solution.py:98
  313.3 1.2 convert_bitcast_fusion
  314.4 0.7 slice.18
  315.1 0.7 slice.19
  (2 shorter events, 0.1 us)
Async XLA Ops:
  7.2 57.0 %all-gather.2.cloned.1.call-start = ((), (), s32[]{:S(2)}) async-start(), calls=%async_computation.2 | async-start | bytes 6684672 | tf_op jit(solution)/shard_map/all_gather | solution.py:64
  81.9 2.7 copy-start
  85.3 14.8 %all-to-all-start = ((f32[8,2,2048]{2,1,0:T(2,128)}), f32[8,2,2048]{2,1,0:T(2,128)S(1)}, u32[]{:S(2)}, u32[]{:S(2)}) async-start(f32[8,2,2048]{2,1,0:T(2,128)} %stack.2), calls=%async_computation | async-start | bytes 262144 | tf_op jit(solution)/shard_map/all_to_all | solution.py:81
  92.2 117.6 %all-reduce.3.cloned.1.call-start = ((), (), s32[]{:S(2)}) async-start(), calls=%async_computation.4 | async-start | bytes 262144
  129.6 183.7 %reduce-scatter.2.cloned.1.call-start = ((), (), s32[]{:S(2)}) async-start(), calls=%async_computation.3 | async-start | bytes 13369344 | tf_op jit(solution)/shard_map/reduce_scatter | solution.py:98
Sparse Core Ops, SparseCore 0:
  9.6 54.5 all-gather.1
  129.7 79.9 all-reduce.2
  233.2 80.0 reduce-scatter.1
